TPU v7x, 256 devices: a whole 4x4x8 slice. The times are simulated.
256 devices in a mesh: row: 16 (over x_lo, y, core), col: 16 (over z, x_hi).
Axes of the slice: x: 4 (x_hi: 2, x_lo: 2; x = x_hi * 2 + x_lo), y: 4, z: 8, core: 2. Of those that a mesh axis runs over, the one named last changes fastest.
Arguments:
- features: bfloat16 [65536, 128], P(('col', 'row')), may hold values from -6 to 6
- weight: bfloat16 [128, 256], replicated, may hold values from -0.5 to 0.5
- adj_tiles: bfloat16 [16, 16, 384, 128, 128], P('row', 'col'), may hold values from -0.125 to 0.125
- tile_row: int32 [16, 16, 384], P('row', 'col'), may hold values from 0 to 31
- tile_col: int32 [16, 16, 384], P('row', 'col'), may hold values from 0 to 31
- tile_count: int32 [16, 16], P('row', 'col'), may hold values from 48 to 384, as said below
- cotangent: bfloat16 [65536, 256], P(('row', 'col')), may hold values from -6 to 6
Outputs:
- activations: bfloat16 [65536, 256], P(('row', 'col'))
- feature_grad: bfloat16 [65536, 128], P(('col', 'row'))
- weight_grad: float32 [128, 256], replicated
Inputs may be any that keep to these rules, and one draw needn't show every extreme that they name: `tile_count`: tiles in use on a device; some device uses all 384 slots.
All inputs are finite; a program needn't handle non-finite values.
Results may differ from a plain program's by a relative error of at most 0.023.
Values may be sent and summed in bfloat16 or wider, within the bound.
A program may use at most 128 MiB of HBM per device.

v0:
```python
import math

import jax
import jax.numpy as jnp
from jax import lax
from jax.sharding import PartitionSpec as P


def tile_sum(adj_block, lead_idx, trail_idx, tile_total, source, out_blocks, forward):
    total_slots = adj_block.shape[0]
    side = adj_block.shape[1]
    width = source.shape[2]
    block_len = math.gcd(64, total_slots)
    picked_idx = trail_idx if forward else lead_idx
    placed_idx = lead_idx if forward else trail_idx
    pattern = "tij,tjf->tif" if forward else "tji,tjf->tif"

    def one_block(turn_idx, summed):
        offset = turn_idx * block_len
        chosen = lax.dynamic_slice_in_dim(adj_block, offset, block_len, 0)
        picked = lax.dynamic_slice_in_dim(picked_idx, offset, block_len, 0)
        placed = lax.dynamic_slice_in_dim(placed_idx, offset, block_len, 0)
        gathered = jnp.take(source, picked, axis=0)
        products = jnp.einsum(pattern, chosen, gathered, preferred_element_type=jnp.float32)
        alive_mask = (offset + jnp.arange(block_len, dtype=jnp.int32) < tile_total).astype(
            jnp.float32
        )
        return summed.at[placed].add(products * alive_mask[:, None, None])

    initial = jnp.zeros((out_blocks, side, width), jnp.float32)
    turns = total_slots // block_len
    return lax.fori_loop(0, turns, one_block, initial)


def swish_parts(preact):
    sigma = jax.nn.sigmoid(preact)
    return (preact * sigma, sigma * (1.0 + preact * (1.0 - sigma)))


def body(features, weight, adj_tiles, tile_row, tile_col, tile_count, cotangent):
    adj_block = adj_tiles[0, 0]
    lead_idx = tile_row[0, 0]
    trail_idx = tile_col[0, 0]
    tile_total = tile_count[0, 0]
    side = adj_block.shape[1]
    width = features.shape[1]
    piece = cotangent.shape[0]
    col_devices = lax.axis_size("col")
    row_nodes = piece * col_devices
    nodes = row_nodes * lax.axis_size("row")
    column_feats = lax.all_gather(features, "row", axis=0, tiled=True)
    col_count = column_feats.shape[0] // side
    partial_value = tile_sum(
        adj_block,
        lead_idx,
        trail_idx,
        tile_total,
        column_feats.reshape(col_count, side, width),
        row_nodes // side,
        True,
    )
    partial_value = partial_value.reshape(row_nodes, width)
    offset = lax.axis_index("col") * piece
    summed = lax.psum(partial_value, "col")
    aggregated = summed.astype(jnp.bfloat16)
    preact = jnp.dot(aggregated, weight, preferred_element_type=jnp.float32)
    output_all, slope = swish_parts(preact)
    activations = lax.dynamic_slice_in_dim(output_all, offset, piece, 0).astype(jnp.bfloat16)
    cot_group = lax.all_gather(cotangent, "col", axis=0, tiled=True)
    pre_grad = (cot_group.astype(jnp.float32) * slope).astype(jnp.bfloat16)
    own_agg = lax.dynamic_slice_in_dim(aggregated, offset, piece, 0)
    own_grad = lax.dynamic_slice_in_dim(pre_grad, offset, piece, 0)
    weight_terms = lax.dot_general(
        own_agg, own_grad, (((0,), (0,)), ((), ())), preferred_element_type=jnp.float32
    )
    agg_group = lax.dot_general(
        pre_grad, weight, (((1,), (1,)), ((), ())), preferred_element_type=jnp.float32
    ).astype(jnp.bfloat16)
    weight_grad = lax.psum(weight_terms, ("row", "col")) / math.sqrt(nodes)
    adjoint = tile_sum(
        adj_block,
        lead_idx,
        trail_idx,
        tile_total,
        agg_group.reshape(row_nodes // side, side, width),
        col_count,
        False,
    )
    adjoint = adjoint.reshape(col_count * side, width)
    feature_grad = lax.psum_scatter(
        adjoint.astype(jnp.bfloat16), "row", scatter_dimension=0, tiled=True
    )
    return (activations, feature_grad, weight_grad)


def solution(mesh):
    in_specs = (
        P(("col", "row"), None),
        P(),
        P("row", "col", None, None, None),
        P("row", "col", None),
        P("row", "col", None),
        P("row", "col"),
        P(("row", "col"), None),
    )
    out_specs = (P(("row", "col"), None), P(("col", "row"), None), P())
    return jax.shard_map(body, mesh=mesh, in_specs=in_specs, out_specs=out_specs, check_vma=False)
```

profile of v0, /device:TPU:1, one launch (start us, length us, event | category | flops | bytes accessed | tf_op | source)
XLA Modules:
  0.0 576.9 jit_solution(11565442216682452234)
XLA Ops:
  10.1 16.6 %copy.10 = bf16[1,1,384,128,128]{3,4,2,1,0:T(8,128)(2,1)} copy(bf16[1,1,384,128,128]{4,3,2,1,0:T(8,128)(2,1)} %param.15) | data formatting | bytes 25165824 | tf_op args[2]
  26.7 22.4 %all-gather.3.cloned.1.call-done = bf16[4096,128]{1,0:T(8,128)(2,1)} async-done(((bf16[256,128]{1,0:T(8,128)(2,1)}), bf16[4096,128]{1,0:T(8,128)(2,1)}) %all-gather.3.cloned.1.call-update) | async-done | bytes 1048592 | tf_op jit(solution)/shard_map/all_gather | solution.py:51
  50.3 100.7 %while.26 = (s32[]{:T(128)}, f32[32,128,128]{2,1,0:T(8,128)S(1)}, s32[384]{0:T(512)S(1)}, bf16[384,128,128]{2,1,0:T(8,128)(2,1)}, s32[384]{0:T(512)S(1)}, /*inde...) while((s32[]{:T(128)}, f32[32,128,128]{2,1,0:T(8,128)S(1)}, ...), condition=%wide.region_2.0_spmd, body=%wide.region_0.3_spmd.sunk | while | flops 271582976 | bytes 25172528 | solution.py:32
  58.2 8.8 %scatter_fusion = f32[32,128,128]{2,1,0:T(8,128)S(1)} fusion(f32[32,128,128]{2,1,0:T(8,128)S(1)} %get-tuple-element.408, s32[64]{0:T(128)S(1)} %compare_select_fusion.8, f32[64,128,128]{2,1,0:T(8,128)} %convolution_multiply_fusion.4), kind=kCustom, calls=%fused_computation.2.clone.1 | custom fusion | flops 1048576 | bytes 12583168 | tf_op jit(solution)/shard_map/while/body/eval_jaxpr/scatter-add | solution.py:28
  75.0 8.8 %scatter_fusion = f32[32,128,128]{2,1,0:T(8,128)S(1)} fusion(f32[32,128,128]{2,1,0:T(8,128)S(1)} %get-tuple-element.408, s32[64]{0:T(128)S(1)} %compare_select_fusion.8, f32[64,128,128]{2,1,0:T(8,128)} %convolution_multiply_fusion.4), kind=kCustom, calls=%fused_computation.2.clone.1 | custom fusion | flops 1048576 | bytes 12583168 | tf_op jit(solution)/shard_map/while/body/eval_jaxpr/scatter-add | solution.py:28
  91.8 8.8 %scatter_fusion = f32[32,128,128]{2,1,0:T(8,128)S(1)} fusion(f32[32,128,128]{2,1,0:T(8,128)S(1)} %get-tuple-element.408, s32[64]{0:T(128)S(1)} %compare_select_fusion.8, f32[64,128,128]{2,1,0:T(8,128)} %convolution_multiply_fusion.4), kind=kCustom, calls=%fused_computation.2.clone.1 | custom fusion | flops 1048576 | bytes 12583168 | tf_op jit(solution)/shard_map/while/body/eval_jaxpr/scatter-add | solution.py:28
  108.6 8.8 %scatter_fusion = f32[32,128,128]{2,1,0:T(8,128)S(1)} fusion(f32[32,128,128]{2,1,0:T(8,128)S(1)} %get-tuple-element.408, s32[64]{0:T(128)S(1)} %compare_select_fusion.8, f32[64,128,128]{2,1,0:T(8,128)} %convolution_multiply_fusion.4), kind=kCustom, calls=%fused_computation.2.clone.1 | custom fusion | flops 1048576 | bytes 12583168 | tf_op jit(solution)/shard_map/while/body/eval_jaxpr/scatter-add | solution.py:28
  120.3 5.0 convolution_multiply_fusion.4
  125.4 8.8 %scatter_fusion = f32[32,128,128]{2,1,0:T(8,128)S(1)} fusion(f32[32,128,128]{2,1,0:T(8,128)S(1)} %get-tuple-element.408, s32[64]{0:T(128)S(1)} %compare_select_fusion.8, f32[64,128,128]{2,1,0:T(8,128)} %convolution_multiply_fusion.4), kind=kCustom, calls=%fused_computation.2.clone.1 | custom fusion | flops 1048576 | bytes 12583168 | tf_op jit(solution)/shard_map/while/body/eval_jaxpr/scatter-add | solution.py:28
  142.2 8.8 %scatter_fusion = f32[32,128,128]{2,1,0:T(8,128)S(1)} fusion(f32[32,128,128]{2,1,0:T(8,128)S(1)} %get-tuple-element.408, s32[64]{0:T(128)S(1)} %compare_select_fusion.8, f32[64,128,128]{2,1,0:T(8,128)} %convolution_multiply_fusion.4), kind=kCustom, calls=%fused_computation.2.clone.1 | custom fusion | flops 1048576 | bytes 12583168 | tf_op jit(solution)/shard_map/while/body/eval_jaxpr/scatter-add | solution.py:28
  151.0 100.8 %all-reduce.4 = bf16[4096,128]{1,0:T(8,128)(2,1)S(1)} all-reduce(f32[4096,128]{1,0:T(8,128)S(1)} %bitcast.11), channel_id=1, replica_groups=mesh['row'=16,'col'=16] {'col'}, use_global_device_ids=true, to_apply=%region_3.5 | all-reduce | flops 524288 | bytes 3145728 | tf_op jit(solution)/shard_map/psum | solution.py:64
  251.9 6.8 %multiply_convert_fusion = (bf16[4096,256]{1,0:T(8,128)(2,1)S(1)}, f32[4096,256]{1,0:T(8,128)}, f32[4096,256]{1,0:T(8,128)}) fusion(bf16[4096,256]{1,0:T(8,128)(2,1)} %all-gather.5.cloned.1.call-done, bf16[4096,128]{1,0:T(8,128)(2,1)S(1)} %all-reduce.4, bf16[128,256]{1,0:T(8,128)(2,1)S(1)} %copy-done), kind=kOutput, calls=%fused_computation.29 | convolution fusion | flops 278921216 | bytes 13697024 | tf_op jit(solution)/shard_map/dot_general | solution.py:66
  261.4 101.1 %while.27 = (s32[]{:T(128)}, f32[32,128,128]{2,1,0:T(8,128)S(1)}, s32[384]{0:T(512)S(1)}, bf16[384,128,128]{1,2,0:T(8,128)(2,1)}, s32[384]{0:T(512)S(1)}, /*inde...) while((s32[]{:T(128)}, f32[32,128,128]{2,1,0:T(8,128)S(1)}, ...), condition=%wide.region_6.8_spmd, body=%wide.region_4.0_spmd.sunk | while | flops 271582976 | bytes 25172528 | solution.py:32
  269.4 8.8 %scatter_fusion.1 = f32[32,128,128]{2,1,0:T(8,128)S(1)} fusion(f32[32,128,128]{2,1,0:T(8,128)S(1)} %get-tuple-element.441, s32[64]{0:T(128)S(1)} %compare_select_fusion.9, f32[64,128,128]{2,1,0:T(8,128)} %convolution_multiply_fusion.5), kind=kCustom, calls=%fused_computation.3.clone.1 | custom fusion | flops 1048576 | bytes 12583168 | tf_op jit(solution)/shard_map/while/body/eval_jaxpr/scatter-add | solution.py:28
  281.2 5.0 convolution_multiply_fusion.5
  286.2 8.8 %scatter_fusion.1 = f32[32,128,128]{2,1,0:T(8,128)S(1)} fusion(f32[32,128,128]{2,1,0:T(8,128)S(1)} %get-tuple-element.441, s32[64]{0:T(128)S(1)} %compare_select_fusion.9, f32[64,128,128]{2,1,0:T(8,128)} %convolution_multiply_fusion.5), kind=kCustom, calls=%fused_computation.3.clone.1 | custom fusion | flops 1048576 | bytes 12583168 | tf_op jit(solution)/shard_map/while/body/eval_jaxpr/scatter-add | solution.py:28
  303.1 8.8 %scatter_fusion.1 = f32[32,128,128]{2,1,0:T(8,128)S(1)} fusion(f32[32,128,128]{2,1,0:T(8,128)S(1)} %get-tuple-element.441, s32[64]{0:T(128)S(1)} %compare_select_fusion.9, f32[64,128,128]{2,1,0:T(8,128)} %convolution_multiply_fusion.5), kind=kCustom, calls=%fused_computation.3.clone.1 | custom fusion | flops 1048576 | bytes 12583168 | tf_op jit(solution)/shard_map/while/body/eval_jaxpr/scatter-add | solution.py:28
  314.9 5.0 convolution_multiply_fusion.5
  319.9 8.8 %scatter_fusion.1 = f32[32,128,128]{2,1,0:T(8,128)S(1)} fusion(f32[32,128,128]{2,1,0:T(8,128)S(1)} %get-tuple-element.441, s32[64]{0:T(128)S(1)} %compare_select_fusion.9, f32[64,128,128]{2,1,0:T(8,128)} %convolution_multiply_fusion.5), kind=kCustom, calls=%fused_computation.3.clone.1 | custom fusion | flops 1048576 | bytes 12583168 | tf_op jit(solution)/shard_map/while/body/eval_jaxpr/scatter-add | solution.py:28
  331.7 5.0 convolution_multiply_fusion.5
  336.8 8.8 %scatter_fusion.1 = f32[32,128,128]{2,1,0:T(8,128)S(1)} fusion(f32[32,128,128]{2,1,0:T(8,128)S(1)} %get-tuple-element.441, s32[64]{0:T(128)S(1)} %compare_select_fusion.9, f32[64,128,128]{2,1,0:T(8,128)} %convolution_multiply_fusion.5), kind=kCustom, calls=%fused_computation.3.clone.1 | custom fusion | flops 1048576 | bytes 12583168 | tf_op jit(solution)/shard_map/while/body/eval_jaxpr/scatter-add | solution.py:28
  353.6 8.8 %scatter_fusion.1 = f32[32,128,128]{2,1,0:T(8,128)S(1)} fusion(f32[32,128,128]{2,1,0:T(8,128)S(1)} %get-tuple-element.441, s32[64]{0:T(128)S(1)} %compare_select_fusion.9, f32[64,128,128]{2,1,0:T(8,128)} %convolution_multiply_fusion.5), kind=kCustom, calls=%fused_computation.3.clone.1 | custom fusion | flops 1048576 | bytes 12583168 | tf_op jit(solution)/shard_map/while/body/eval_jaxpr/scatter-add | solution.py:28
  365.4 143.8 %all-reduce.3.cloned.1.call-done = f32[128,256]{1,0:T(8,128)} async-done(((f32[128,256]{1,0:T(8,128)}), f32[128,256]{1,0:T(8,128)}) %all-reduce.3.cloned.1.call-update) | async-done | bytes 131088 | tf_op jit(solution)/shard_map/psum | solution.py:79
  510.8 59.6 %reduce-scatter.2.cloned.1.call-done = bf16[256,128]{1,0:T(8,128)(2,1)} async-done(((bf16[4096,128]{1,0:T(8,128)(2,1)}), bf16[256,128]{1,0:T(8,128)(2,1)}) %reduce-scatter.2.cloned.1.call-update) | async-done | bytes 65552 | tf_op jit(solution)/shard_map/reduce_scatter | solution.py:90
  (80 shorter events, 87.0 us)
Async XLA Ops:
  7.2 244.7 %copy-start = (bf16[128,256]{1,0:T(8,128)(2,1)S(1)}, bf16[128,256]{1,0:T(8,128)(2,1)}, u32[]{:S(2)}) copy-start(bf16[128,256]{1,0:T(8,128)(2,1)} %param.14) | copy-start | bytes 196612
  7.2 41.9 %all-gather.3.cloned.1.call-start = ((), (), s32[]{:S(2)}) async-start(), calls=%async_computation.1 | async-start | bytes 1114112 | tf_op jit(solution)/shard_map/all_gather | solution.py:51
  7.9 244.0 %all-gather.5.cloned.1.call-start = ((), (), s32[]{:S(2)}) async-start(), calls=%async_computation.2 | async-start | bytes 2228224 | tf_op jit(solution)/shard_map/all_gather | solution.py:69
  8.7 500.5 %all-reduce.3.cloned.1.call-start = ((), (), s32[]{:S(2)}) async-start(), calls=%async_computation.4 | async-start | bytes 262144 | tf_op jit(solution)/shard_map/psum | solution.py:79
  49.1 1.2 copy-start.1
  251.8 6.8 %copy-start.2 = (bf16[4096,128]{1,0:T(8,128)(2,1)}, bf16[4096,128]{1,0:T(8,128)(2,1)S(1)}, u32[]{:S(2)}) copy-start(bf16[4096,128]{1,0:T(8,128)(2,1)S(1)} %all-reduce.4) | copy-start | bytes 3145732
  261.1 309.3 %reduce-scatter.2.cloned.1.call-start = ((), (), s32[]{:S(2)}) async-start(), calls=%async_computation.3 | async-start | bytes 1114112 | tf_op jit(solution)/shard_map/reduce_scatter | solution.py:90
Sparse Core Ops, SparseCore 0:
  9.9 39.1 all-gather.2
  51.7 81.5 all-gather.4
  261.2 247.9 all-reduce.2
  512.1 58.1 reduce-scatter.1
where the time goes:
time: 582 us; the launch traced here: 577 us
  waiting for transfers between devices  227 us (39%)
  other arithmetic  121 us (21%)
  blocking collectives  101 us (17%)
  matrix products  69 us (12%)
  local copies, waits for them, and re-layouts  44.3 us (8%)
  between operations  13.8 us (2%)
    psum x1, waiting for transfers between devices, body(): weight_grad = lax.psum(weight_terms, ('row', 'col')) / math.sqrt(nodes)  144 us
    scatter-add x12, other arithmetic, one_block(): return summed.at[placed].add(products * alive_mask[:, None, None])  106 us
    psum x1, blocking collectives, body(): summed = lax.psum(partial_value, 'col')  101 us
    dot_general x12, matrix products, one_block(): jnp.einsum(pattern, chosen, gathered, preferred_element_type=jnp.float32)  59.8 us
    reduce_scatter x1, waiting for transfers between devices, body(): lax.psum_scatter(adjoint.astype(jnp.bfloat16), 'row', scatter_dimension=0...  59.6 us
    gather x12, local copies, waits for them, and re-layouts, one_block(): gathered = jnp.take(source, picked, axis=0)  26.2 us
    all_gather x1, waiting for transfers between devices, body(): column_feats = lax.all_gather(features, 'row', axis=0, tiled=True)  22.4 us
    unnamed x7, local copies, waits for them, and re-layouts  17.6 us
  transfers between devices with their start and end apart: 4, of which 3 were waited for; matrix products, arithmetic and copies ran while one was open for 39% of the time, Pallas kernels for 0%

commit v1 on v0

v1 whole, which is shorter than its diff:
```python
import math

import jax
import jax.numpy as jnp
from jax import lax
from jax.experimental import pallas as pl
from jax.experimental.pallas import tpu as pltpu
from jax.sharding import PartitionSpec as P

F32 = jnp.float32
BF16 = jnp.bfloat16
MESH = pl.DeviceIdType.MESH

SIDE = 128
BLOCKS = 32
SLOTS = 384
PAIRS = (SLOTS + BLOCKS) // 2
ENTRIES = 512
GROUP = 16
UNROLL = 16
LOADS = 8
ZERO = BLOCKS
TILE, SOURCE, KEEP, LAST, SOME = range(5)


def upright(flat, lanes):
    column = jnp.transpose(jnp.broadcast_to(flat, (SIDE, flat.shape[1])))
    return jnp.concatenate([column] * (lanes // SIDE), axis=1)


def over_rows(condition, value):
    return jnp.sum(jnp.where(condition, value, 0), axis=0, keepdims=True)


def plan_pairs(place, pick, total):
    def counts(shape):
        return [lax.broadcasted_iota(jnp.int32, shape, d) for d in range(2)]

    place_up = upright(place, SLOTS)
    down, across = counts((SLOTS, SLOTS))
    rank = over_rows((place_up == place) & (down < total) & (down < across), 1)
    down, across = counts((SLOTS, SIDE))
    tiles = over_rows((place_up[:, :SIDE] == across) & (down < total), 1)
    pairs = (tiles + 1) // 2
    pairs_up = upright(pairs, SIDE)
    down, across = counts((SIDE, SIDE))
    first = over_rows(down < across, pairs_up)
    first_up = upright(first, ENTRIES)
    down, across = counts((BLOCKS, SLOTS))
    spot = rank + 2 * over_rows(down == place, first_up[:BLOCKS, :SLOTS])
    spot = jnp.where(lax.broadcasted_iota(jnp.int32, (1, SLOTS), 1) < total, spot, -1)
    down, across = counts((SLOTS, ENTRIES))
    found = upright(spot, ENTRIES) == across
    tile = over_rows(found, down)
    source = over_rows(found, upright(pick, ENTRIES) - ZERO) + ZERO
    down, across = counts((BLOCKS, ENTRIES))
    pairs_up = jnp.concatenate([pairs_up[:BLOCKS]] * (ENTRIES // SIDE), axis=1)
    keep = 1 - over_rows((first_up[:BLOCKS] == across) & (pairs_up > 0), 1)
    return tile, source, keep, jnp.maximum(first + pairs - 1, 0), jnp.minimum(pairs, 1)


def kernel(
    feat_hbm, weight_hbm, adj_hbm, row_hbm, col_hbm, count_hbm, cot_hbm,
    act_hbm, fgrad_hbm, wgrad_hbm,
    tiles, sums, xs, gs, weight, cot, rows, cols, plan_v, act_v, fgrad_v,
    col_out, col_in, col_sum, col_land, row_out, row_in, row_sum, row_land,
    wt, wt_land, wpart, wpart_land, wgrad_v,
    plan_f, plan_b, count,
    load_sem, small_sem, plan_sem, out_sem,
    ag1_send, ag1_recv, ag1f_send, ag1f_recv,
    rsx_send, rsx_recv, rsz_send, rsz_recv,
    ag2_send, ag2_recv, ag2f_send, ag2f_recv,
    rsc_send, rsc_recv, rsr_send, rsr_recv,
    w1_send, w1_recv, w2_send, w2_recv, w3_send, w3_recv,
):
    r = lax.axis_index("row")
    c = lax.axis_index("col")
    core, chip = r % 2, r // 2
    xlo, y = chip // 4, chip % 4
    xhi, z = c % 2, c // 2
    sibling = (2 * chip + (1 - core), c)
    partner = (r, 2 * z + (1 - xhi))

    def chip_at(k, sign):
        return 4 * ((xlo + k // 4) % 2) + (y + sign * (k % 4) + 4) % 4

    def z_at(k, sign):
        return (z + sign * k + 8) % 8

    def remote(src, dst, send, recv, device):
        return pltpu.make_async_remote_copy(
            src_ref=src, dst_ref=dst, send_sem=send, recv_sem=recv,
            device_id=device, device_id_type=MESH,
        )

    barrier = pltpu.get_barrier_semaphore()
    for k in range(1, GROUP):
        pl.semaphore_signal(barrier, inc=1, device_id=((r + k) % GROUP, c), device_id_type=MESH)
        pl.semaphore_signal(barrier, inc=1, device_id=(r, (c + k) % GROUP), device_id_type=MESH)

    smalls = [
        pltpu.make_async_copy(row_hbm.at[0, 0], rows.at[0], small_sem.at[0]),
        pltpu.make_async_copy(col_hbm.at[0, 0], cols.at[0], small_sem.at[1]),
        pltpu.make_async_copy(count_hbm, count, small_sem.at[2]),
        pltpu.make_async_copy(feat_hbm, xs.at[pl.ds(2 * r, 2)], small_sem.at[3]),
        pltpu.make_async_copy(weight_hbm, weight, small_sem.at[4]),
        pltpu.make_async_copy(cot_hbm, cot, small_sem.at[5]),
    ]
    for copy in smalls:
        copy.start()
    part = SLOTS // LOADS
    loads = [
        pltpu.make_async_copy(
            adj_hbm.at[0, 0, pl.ds(i * part, part)], tiles.at[pl.ds(i * part, part)], load_sem.at[i]
        )
        for i in range(LOADS)
    ]
    for copy in loads:
        copy.start()
    xs[ZERO] = jnp.zeros((SIDE, SIDE), BF16)
    gs[ZERO] = jnp.zeros((SIDE, SIDE), BF16)
    pl.semaphore_wait(barrier, 2 * (GROUP - 1))

    pending = []
    here = pl.ds(2 * r, 2)
    for k in range(8):
        device = sibling if k == 0 else (2 * chip_at(k, 1) + core, c)
        copy = remote(feat_hbm, xs.at[here], ag1_send.at[k], ag1_recv.at[k], device)
        copy.start()
        pending.append(copy)

    for copy in smalls[:3]:
        copy.wait()
    total = count[0, 0]
    plan_v[...] = jnp.zeros_like(plan_v)
    for i, (place, pick, ready) in enumerate(((rows, cols, plan_f), (cols, rows, plan_b))):
        listed = plan_pairs(place[...], pick[...], total)
        for j, value in enumerate(listed):
            plan_v[i, j : j + 1, : value.shape[1]] = value
        pltpu.make_async_copy(plan_v.at[i], ready, plan_sem.at[i]).start()

    forwards = []
    for k in range(1, 8):
        slot = xs.at[pl.ds(2 * (2 * chip_at(k, -1) + core), 2)]
        remote(slot, slot, ag1_send.at[k], ag1_recv.at[k], sibling).wait_recv()
        copy = remote(slot, slot, ag1f_send.at[k - 1], ag1f_recv.at[k - 1], sibling)
        copy.start()
        forwards.append(copy)
    slot = xs.at[pl.ds(2 * (2 * chip + 1 - core), 2)]
    remote(slot, slot, ag1_send.at[0], ag1_recv.at[0], sibling).wait_recv()
    for k in range(1, 8):
        slot = xs.at[pl.ds(2 * (2 * chip_at(k, -1) + 1 - core), 2)]
        remote(slot, slot, ag1f_send.at[k - 1], ag1f_recv.at[k - 1], sibling).wait_recv()
    for copy in smalls[3:]:
        copy.wait()
    for i in range(2):
        pltpu.make_async_copy(plan_v.at[i], (plan_f, plan_b)[i], plan_sem.at[i]).wait()
    for copy in loads:
        copy.wait()
    for copy in pending + forwards:
        copy.wait_send()

    def tile_pass(listed, source, forward):
        def some_pairs(turn, total):
            for u in range(UNROLL):
                p = turn * UNROLL + u
                one, two = tiles[listed[TILE, 2 * p]], tiles[listed[TILE, 2 * p + 1]]
                with_one, with_two = source[listed[SOURCE, 2 * p]], source[listed[SOURCE, 2 * p + 1]]
                if forward:
                    left = jnp.concatenate([one, two], axis=1)
                    right = jnp.concatenate([with_one, with_two], axis=0)
                else:
                    left = jnp.concatenate([with_one, with_two], axis=1)
                    right = jnp.concatenate([one, two], axis=0)
                product = jnp.dot(left, right, preferred_element_type=F32)
                total = total * listed[KEEP, p].astype(F32) + product
                sums[p] = total
            return total

        lax.fori_loop(0, PAIRS // UNROLL, some_pairs, jnp.zeros((SIDE, SIDE), F32))

    def block_sum(listed, b):
        return sums[listed[LAST, b]] * listed[SOME, b].astype(F32)

    tile_pass(plan_f, xs, True)
    order = (4, 3, 5, 2, 6, 1, 7, 0)
    pending = []
    for k in order:
        for h in range(2):
            b = 2 * (2 * z_at(k, 1) + 1 - xhi) + h
            col_out[k, h] = block_sum(plan_f, b).astype(BF16)
        copy = remote(col_out.at[k], col_in.at[k], rsx_send.at[k], rsx_recv.at[k], partner)
        copy.start()
        pending.append(copy)
    own = []
    for k in order:
        mine = [block_sum(plan_f, 2 * (2 * z_at(k, 1) + xhi) + h) for h in range(2)]
        remote(col_in.at[k], col_in.at[k], rsx_send.at[k], rsx_recv.at[k], partner).wait_recv()
        mine = [mine[h] + col_in[k, h].astype(F32) for h in range(2)]
        if k == 0:
            own = mine
        else:
            for h in range(2):
                col_sum[k, h] = mine[h].astype(BF16)
            copy = remote(
                col_sum.at[k], col_land.at[k], rsz_send.at[k - 1], rsz_recv.at[k - 1],
                (r, 2 * z_at(k, 1) + xhi),
            )
            copy.start()
            pending.append(copy)
    for k in (1, 7, 2, 6, 3, 5, 4):
        remote(
            col_land.at[k], col_land.at[k], rsz_send.at[k - 1], rsz_recv.at[k - 1], partner
        ).wait_recv()
        own = [own[h] + col_land[k, h].astype(F32) for h in range(2)]

    aggregated = jnp.concatenate(own, axis=0).astype(BF16)
    w = weight[...]
    preact = jnp.dot(aggregated, w, preferred_element_type=F32)
    sigma = jax.nn.sigmoid(preact)
    slope = sigma * (1.0 + preact * (1.0 - sigma))
    pre_grad = (cot[...].astype(F32) * slope).astype(BF16)
    agg_grad = lax.dot_general(
        w, pre_grad, (((1,), (1,)), ((), ())), preferred_element_type=F32
    ).astype(BF16)
    for h in range(2):
        gs[2 * c + h] = agg_grad[:, h * SIDE : (h + 1) * SIDE]

    here = pl.ds(2 * c, 2)
    ahead = (1, 7, 2, 6, 3, 5, 4)
    for k in ahead:
        copy = remote(
            gs.at[here], gs.at[here], ag2_send.at[k], ag2_recv.at[k], (r, 2 * z_at(k, 1) + xhi)
        )
        copy.start()
        pending.append(copy)
    copy = remote(gs.at[here], gs.at[here], ag2_send.at[0], ag2_recv.at[0], partner)
    copy.start()
    pending.append(copy)

    act_v[...] = (preact * sigma).astype(BF16)
    act_out = pltpu.make_async_copy(act_v, act_hbm, out_sem.at[0])
    act_out.start()
    terms = lax.dot_general(
        aggregated, pre_grad, (((0,), (0,)), ((), ())), preferred_element_type=F32
    )
    for q in range(GROUP):
        wt[q] = terms[8 * q : 8 * q + 8]
    for k in range(1, GROUP):
        to = (c + k) % GROUP
        copy = remote(wt.at[to], wt_land.at[k], w1_send.at[k], w1_recv.at[k], (r, to))
        copy.start()
        pending.append(copy)

    for k in ahead:
        slot = gs.at[pl.ds(2 * (2 * z_at(k, -1) + xhi), 2)]
        remote(slot, slot, ag2_send.at[k], ag2_recv.at[k], partner).wait_recv()
        copy = remote(slot, slot, ag2f_send.at[k - 1], ag2f_recv.at[k - 1], partner)
        copy.start()
        pending.append(copy)
    term = wt[c]
    for k in range(1, GROUP):
        remote(wt_land.at[k], wt_land.at[k], w1_send.at[k], w1_recv.at[k], partner).wait_recv()
        term = term + wt_land[k]
    wpart[...] = term
    for k in range(1, GROUP):
        copy = remote(
            wpart, wpart_land.at[k], w2_send.at[k], w2_recv.at[k], ((r + k) % GROUP, c)
        )
        copy.start()
        pending.append(copy)
    slot = gs.at[pl.ds(2 * (2 * z + 1 - xhi), 2)]
    remote(slot, slot, ag2_send.at[0], ag2_recv.at[0], partner).wait_recv()
    for k in ahead:
        slot = gs.at[pl.ds(2 * (2 * z_at(k, -1) + 1 - xhi), 2)]
        remote(slot, slot, ag2f_send.at[k - 1], ag2f_recv.at[k - 1], partner).wait_recv()

    tile_pass(plan_b, gs, False)
    order = (2, 6, 1, 3, 5, 7, 4, 0)
    for k in order:
        for h in range(2):
            b = 2 * (2 * chip_at(k, 1) + 1 - core) + h
            row_out[k, h] = block_sum(plan_b, b).astype(BF16)
        copy = remote(row_out.at[k], row_in.at[k], rsc_send.at[k], rsc_recv.at[k], sibling)
        copy.start()
        pending.append(copy)
    for k in order:
        mine = [block_sum(plan_b, 2 * (2 * chip_at(k, 1) + core) + h) for h in range(2)]
        remote(row_in.at[k], row_in.at[k], rsc_send.at[k], rsc_recv.at[k], sibling).wait_recv()
        mine = [mine[h] + row_in[k, h].astype(F32) for h in range(2)]
        if k == 0:
            own = mine
        else:
            for h in range(2):
                row_sum[k, h] = mine[h].astype(BF16)
            copy = remote(
                row_sum.at[k], row_land.at[k], rsr_send.at[k - 1], rsr_recv.at[k - 1],
                (2 * chip_at(k, 1) + core, c),
            )
            copy.start()
            pending.append(copy)

    term = wpart[...]
    for k in range(1, GROUP):
        remote(wpart_land.at[k], wpart_land.at[k], w2_send.at[k], w2_recv.at[k], partner).wait_recv()
        term = term + wpart_land[k]
    wgrad_v[c] = term * (1.0 / math.sqrt(SIDE * BLOCKS * GROUP))
    for k in range(1, GROUP):
        copy = remote(
            wgrad_v.at[c], wgrad_v.at[c], w3_send.at[k], w3_recv.at[k], (r, (c + k) % GROUP)
        )
        copy.start()
        pending.append(copy)

    for k in (1, 3, 4, 2, 5, 7, 6):
        remote(
            row_land.at[k], row_land.at[k], rsr_send.at[k - 1], rsr_recv.at[k - 1], sibling
        ).wait_recv()
        own = [own[h] + row_land[k, h].astype(F32) for h in range(2)]
    for h in range(2):
        fgrad_v[h * SIDE : (h + 1) * SIDE, :] = own[h].T.astype(BF16)
    fgrad_out = pltpu.make_async_copy(fgrad_v, fgrad_hbm, out_sem.at[1])
    fgrad_out.start()
    for k in range(1, GROUP):
        slot = wgrad_v.at[(c - k + GROUP) % GROUP]
        remote(slot, slot, w3_send.at[k], w3_recv.at[k], partner).wait_recv()
    wgrad_out = pltpu.make_async_copy(wgrad_v, wgrad_hbm, out_sem.at[2])
    wgrad_out.start()
    for copy in pending:
        copy.wait_send()
    act_out.wait()
    fgrad_out.wait()
    wgrad_out.wait()


def body(features, weight, adj_tiles, tile_row, tile_col, tile_count, cotangent):
    nodes, width = features.shape
    hidden = weight.shape[1]
    any_spec = pl.BlockSpec(memory_space=pl.ANY)
    dma = pltpu.SemaphoreType.DMA
    blocks = lambda *lead: pltpu.VMEM((*lead, SIDE, SIDE), BF16)
    act, fgrad, wgrad = pl.pallas_call(
        kernel,
        out_shape=(
            jax.ShapeDtypeStruct((nodes, hidden), BF16),
            jax.ShapeDtypeStruct((nodes, width), BF16),
            jax.ShapeDtypeStruct((GROUP, 8, hidden), F32),
        ),
        in_specs=[any_spec] * 7,
        out_specs=(any_spec,) * 3,
        scratch_shapes=[
            blocks(SLOTS),
            pltpu.VMEM((PAIRS, SIDE, SIDE), F32),
            blocks(BLOCKS + 1),
            blocks(BLOCKS + 1),
            pltpu.VMEM((width, hidden), BF16),
            pltpu.VMEM((nodes, hidden), BF16),
            pltpu.VMEM((1, SLOTS), jnp.int32),
            pltpu.VMEM((1, SLOTS), jnp.int32),
            pltpu.VMEM((2, 8, ENTRIES), jnp.int32),
            pltpu.VMEM((nodes, hidden), BF16),
            pltpu.VMEM((nodes, width), BF16),
            blocks(8, 2), blocks(8, 2), blocks(8, 2), blocks(8, 2),
            blocks(8, 2), blocks(8, 2), blocks(8, 2), blocks(8, 2),
            pltpu.VMEM((GROUP, 8, hidden), F32),
            pltpu.VMEM((GROUP, 8, hidden), F32),
            pltpu.VMEM((8, hidden), F32),
            pltpu.VMEM((GROUP, 8, hidden), F32),
            pltpu.VMEM((GROUP, 8, hidden), F32),
            pltpu.SMEM((8, ENTRIES), jnp.int32),
            pltpu.SMEM((8, ENTRIES), jnp.int32),
            pltpu.SMEM((1, 1), jnp.int32),
            dma((LOADS,)), dma((6,)), dma((2,)), dma((3,)),
            dma((8,)), dma((8,)), dma((7,)), dma((7,)),
            dma((8,)), dma((8,)), dma((7,)), dma((7,)),
            dma((8,)), dma((8,)), dma((7,)), dma((7,)),
            dma((8,)), dma((8,)), dma((7,)), dma((7,)),
            dma((GROUP,)), dma((GROUP,)), dma((GROUP,)),
            dma((GROUP,)), dma((GROUP,)), dma((GROUP,)),
        ],
        compiler_params=pltpu.CompilerParams(
            collective_id=0, has_side_effects=True, vmem_limit_bytes=50 * 1024 * 1024
        ),
    )(
        features.reshape(nodes // SIDE, SIDE, width), weight, adj_tiles,
        tile_row, tile_col, tile_count, cotangent,
    )
    return act, fgrad, wgrad.reshape(weight.shape)


def solution(mesh):
    in_specs = (
        P(("col", "row"), None),
        P(),
        P("row", "col", None, None, None),
        P("row", "col", None),
        P("row", "col", None),
        P("row", "col"),
        P(("row", "col"), None),
    )
    out_specs = (P(("row", "col"), None), P(("col", "row"), None), P())
    return jax.shard_map(body, mesh=mesh, in_specs=in_specs, out_specs=out_specs, check_vma=False)
```

time: 582 us -> 90.3 us (0.16)
  waiting for transfers between devices: 227 us -> 0 us
  other arithmetic: 121 us -> 0 us
  blocking collectives: 101 us -> 0 us
  Pallas kernels: 0 us -> 82.4 us
  matrix products: 69 us -> 0 us
  local copies, waits for them, and re-layouts: 44.3 us -> 5.88 us
  between operations: 13.8 us -> 1.3 us
    psum x1 -> x0, waiting for transfers between devices: 144 us -> none  [body(): weight_grad = lax.psum(weight_terms, ('row', 'col')) / math.sqrt(nodes)]
    scatter-add x12 -> x0, other arithmetic: 106 us -> none  [one_block(): return summed.at[placed].add(products * alive_mask[:, None, None])]
    psum x1 -> x0, blocking collectives: 101 us -> none  [body(): summed = lax.psum(partial_value, 'col')]
    pallas_call x0 -> x1, Pallas kernels: none -> 82.4 us  [body(): pl.pallas_call(kernel, out_shape=(jax.ShapeDtypeStruct((nodes, hidden), B...]
    dot_general x15 -> x0, matrix products: 69 us -> none  [the longest x12 59.8 us: one_block(): jnp.einsum(pattern, chosen, gathered, preferred_element_type=jnp.float32)]
    reduce_scatter x1 -> x0, waiting for transfers between devices: 59.6 us -> none  [body(): lax.psum_scatter(adjoint.astype(jnp.bfloat16), 'row', scatter_dimension=0...]
    gather x12 -> x0, local copies, waits for them, and re-layouts: 26.2 us -> none  [one_block(): gathered = jnp.take(source, picked, axis=0)]
    all_gather x2 -> x0, waiting for transfers between devices: 22.4 us -> none  [the longest x1 22.4 us: body(): column_feats = lax.all_gather(features, 'row', axis=0, tiled=True)]
  transfers between devices with their start and end apart: 4 -> 0, of which waited for: 3 -> 0; matrix products, arithmetic and copies ran while one was open for 39% -> 0% of each run, Pallas kernels for 0% -> 0%
where the time goes in v1:
time: 90.3 us; the launch traced here: 89.6 us
  Pallas kernels  82.4 us (91%)
  local copies, waits for them, and re-layouts  5.88 us (7%)
  between operations  1.3 us (1%)
    pallas_call x1, Pallas kernels, body(): pl.pallas_call(kernel, out_shape=(jax.ShapeDtypeStruct((nodes, hidden), B...  82.4 us
    unnamed x13, local copies, waits for them, and re-layouts  5.88 us

profile of v1, /device:TPU:1, one launch (start us, length us, event | category | flops | bytes accessed | tf_op | source)
XLA Modules:
  0.0 89.6 jit_solution(890686206410123491)
XLA Ops:
  1.3 0.0 copy-start
  1.3 0.9 copy-done
  2.2 0.0 copy-start.1
  2.2 0.8 copy-done.1
  3.0 0.0 copy-start.2
  3.0 0.8 copy-done.2
  3.9 0.0 copy-start.3
  3.9 0.7 copy-done.3
  4.5 0.0 copy-start.4
  4.5 0.7 copy-done.4
  5.2 82.4 %shard_map.94 = (bf16[256,256]{1,0:T(8,128)(2,1)S(1)}, bf16[256,128]{1,0:T(8,128)(2,1)S(1)}, f32[16,8,256]{2,1,0:T(8,128)S(1)}) custom-call(bf16[2,128,128]{2,1,0:T(8,128)(2,1)S(1)} %bitcast.3, bf16[128,256]{1,0:T(8,128)(2,1)S(1)} %copy-done.2, bf16[1,1,384,128,128]{4,3,2,1,0:T(8,128)(2,1)} %adj_hbm.1, s32[1,1,384]{2,1,0:T(1,128)S(1)} %copy-done.3, ...), custom_call_target="tpu_custom_call" | custom-call | tf_op jit(solution)/shard_map/pallas_call | solution.py:342
  87.7 0.7 copy.14
  88.3 0.6 copy.15
  89.0 0.7 copy.16
Async XLA Ops:
  1.3 0.9 %copy-start = (bf16[256,256]{1,0:T(8,128)(2,1)S(1)}, bf16[256,256]{1,0:T(8,128)(2,1)}, u32[]{:S(2)}) copy-start(bf16[256,256]{1,0:T(8,128)(2,1)} %cot_hbm.1) | copy-start | bytes 393220
  2.2 0.8 copy-start.1
  3.0 0.8 copy-start.2
  3.9 0.7 copy-start.3
  4.5 0.7 copy-start.4

commit v2 on v1

--- a/solution.py
+++ b/solution.py
@@ -17,7 +17,9 @@
 PAIRS = (SLOTS + BLOCKS) // 2
 ENTRIES = 512
 GROUP = 16
-UNROLL = 16
+HALF = SIDE // 2
+UNROLL = 26
+TURNS = PAIRS // UNROLL
 LOADS = 8
 ZERO = BLOCKS
 TILE, SOURCE, KEEP, LAST, SOME = range(5)
@@ -62,9 +64,9 @@
 def kernel(
     feat_hbm, weight_hbm, adj_hbm, row_hbm, col_hbm, count_hbm, cot_hbm,
     act_hbm, fgrad_hbm, wgrad_hbm,
-    tiles, sums, xs, gs, weight, cot, rows, cols, plan_v, act_v, fgrad_v,
+    tiles, sums, xs, gs_a, gs_b, weight, cot, rows, cols, plan_v, act_v, fgrad_v,
     col_out, col_in, col_sum, col_land, row_out, row_in, row_sum, row_land,
-    wt, wt_land, wpart, wpart_land, wgrad_v,
+    fgrad_t, wt, wt_land, wpart, wpart_land, wgrad_v,
     plan_f, plan_b, count,
     load_sem, small_sem, plan_sem, out_sem,
     ag1_send, ag1_recv, ag1f_send, ag1f_recv,
@@ -118,7 +120,9 @@
     for copy in loads:
         copy.start()
     xs[ZERO] = jnp.zeros((SIDE, SIDE), BF16)
-    gs[ZERO] = jnp.zeros((SIDE, SIDE), BF16)
+    gs = (gs_a, gs_b)
+    for f in range(2):
+        gs[f][ZERO] = jnp.zeros((HALF, SIDE), BF16)
     pl.semaphore_wait(barrier, 2 * (GROUP - 1))
 
     pending = []
@@ -160,7 +164,10 @@
     for copy in pending + forwards:
         copy.wait_send()
 
-    def tile_pass(listed, source, forward):
+    def tile_pass(listed, source, forward, half=0, service=None):
+        height = SIDE if forward else HALF
+        here = pl.ds(half * HALF, height)
+
         def some_pairs(turn, total):
             for u in range(UNROLL):
                 p = turn * UNROLL + u
@@ -174,13 +181,15 @@
                     right = jnp.concatenate([one, two], axis=0)
                 product = jnp.dot(left, right, preferred_element_type=F32)
                 total = total * listed[KEEP, p].astype(F32) + product
-                sums[p] = total
+                sums[p, here, :] = total
+            if service is not None:
+                service(turn)
             return total
 
-        lax.fori_loop(0, PAIRS // UNROLL, some_pairs, jnp.zeros((SIDE, SIDE), F32))
-
-    def block_sum(listed, b):
-        return sums[listed[LAST, b]] * listed[SOME, b].astype(F32)
+        lax.fori_loop(0, TURNS, some_pairs, jnp.zeros((height, SIDE), F32))
+
+    def block_sum(listed, b, rows=slice(None)):
+        return sums[listed[LAST, b], rows, :] * listed[SOME, b].astype(F32)
 
     tile_pass(plan_f, xs, True)
     order = (4, 3, 5, 2, 6, 1, 7, 0)
@@ -223,20 +232,38 @@
     agg_grad = lax.dot_general(
         w, pre_grad, (((1,), (1,)), ((), ())), preferred_element_type=F32
     ).astype(BF16)
-    for h in range(2):
-        gs[2 * c + h] = agg_grad[:, h * SIDE : (h + 1) * SIDE]
-
-    here = pl.ds(2 * c, 2)
+    for f in range(2):
+        for h in range(2):
+            gs[f][2 * c + h] = agg_grad[f * HALF : (f + 1) * HALF, h * SIDE : (h + 1) * SIDE]
+
+    def nodes_of(at, other):
+        across = 1 - xhi if other else xhi
+        return pl.ds(2 * (2 * at + across), 2)
+
+    def spread(f, k):
+        slot = gs[f].at[nodes_of(z, False)]
+        device = partner if k == 0 else (r, 2 * z_at(k, 1) + xhi)
+        copy = remote(slot, slot, ag2_send.at[f, k], ag2_recv.at[f, k], device)
+        copy.start()
+        pending.append(copy)
+
+    def hand_on(f, k):
+        slot = gs[f].at[nodes_of(z_at(k, -1), False)]
+        remote(slot, slot, ag2_send.at[f, k], ag2_recv.at[f, k], partner).wait_recv()
+        remote(slot, slot, ag2f_send.at[f, k], ag2f_recv.at[f, k], partner).start()
+
+    def gathered(f):
+        slot = gs[f].at[nodes_of(z, True)]
+        remote(slot, slot, ag2_send.at[f, 0], ag2_recv.at[f, 0], partner).wait_recv()
+        for k in ahead:
+            slot = gs[f].at[nodes_of(z_at(k, -1), True)]
+            remote(slot, slot, ag2f_send.at[f, k], ag2f_recv.at[f, k], partner).wait_recv()
+            slot = gs[f].at[nodes_of(z_at(k, -1), False)]
+            pending.append(remote(slot, slot, ag2f_send.at[f, k], ag2f_recv.at[f, k], partner))
+
     ahead = (1, 7, 2, 6, 3, 5, 4)
-    for k in ahead:
-        copy = remote(
-            gs.at[here], gs.at[here], ag2_send.at[k], ag2_recv.at[k], (r, 2 * z_at(k, 1) + xhi)
-        )
-        copy.start()
-        pending.append(copy)
-    copy = remote(gs.at[here], gs.at[here], ag2_send.at[0], ag2_recv.at[0], partner)
-    copy.start()
-    pending.append(copy)
+    for k in ahead + (0,):
+        spread(0, k)
 
     act_v[...] = (preact * sigma).astype(BF16)
     act_out = pltpu.make_async_copy(act_v, act_hbm, out_sem.at[0])
@@ -247,85 +274,105 @@
     for q in range(GROUP):
         wt[q] = terms[8 * q : 8 * q + 8]
     for k in range(1, GROUP):
-        to = (c + k) % GROUP
-        copy = remote(wt.at[to], wt_land.at[k], w1_send.at[k], w1_recv.at[k], (r, to))
+        to = (r + k) % GROUP
+        copy = remote(wt.at[to], wt_land.at[k], w1_send.at[k], w1_recv.at[k], (to, c))
         copy.start()
         pending.append(copy)
 
     for k in ahead:
-        slot = gs.at[pl.ds(2 * (2 * z_at(k, -1) + xhi), 2)]
-        remote(slot, slot, ag2_send.at[k], ag2_recv.at[k], partner).wait_recv()
-        copy = remote(slot, slot, ag2f_send.at[k - 1], ag2f_recv.at[k - 1], partner)
-        copy.start()
-        pending.append(copy)
-    term = wt[c]
+        hand_on(0, k)
+        spread(1, k)
+    spread(1, 0)
+    gathered(0)
+
+    def hand_on_one(turn):
+        @pl.when(turn < 7)
+        def _():
+            step = turn // 2
+            hand_on(1, (1 - turn % 2) * (step + 1) + (turn % 2) * (7 - step))
+
+    def reduce_rows(f):
+        rows = pl.ds(f * HALF, HALF)
+        for k in order:
+            for h in range(2):
+                b = 2 * (2 * chip_at(k, 1) + 1 - core) + h
+                row_out[f, k, h] = block_sum(plan_b, b, rows).astype(BF16)
+            copy = remote(
+                row_out.at[f, k], row_in.at[f, k], rsc_send.at[f, k], rsc_recv.at[f, k], sibling
+            )
+            copy.start()
+            pending.append(copy)
+        for k in order:
+            mine = [block_sum(plan_b, 2 * (2 * chip_at(k, 1) + core) + h, rows) for h in range(2)]
+            remote(
+                row_in.at[f, k], row_in.at[f, k], rsc_send.at[f, k], rsc_recv.at[f, k], sibling
+            ).wait_recv()
+            mine = [mine[h] + row_in[f, k, h].astype(F32) for h in range(2)]
+            if k == 0:
+                for h in range(2):
+                    fgrad_t[h, rows, :] = mine[h]
+            else:
+                for h in range(2):
+                    row_sum[f, k, h] = mine[h].astype(BF16)
+                copy = remote(
+                    row_sum.at[f, k], row_land.at[f, k], rsr_send.at[f, k], rsr_recv.at[f, k],
+                    (2 * chip_at(k, 1) + core, c),
+                )
+                copy.start()
+                pending.append(copy)
+
+    order = (2, 6, 1, 3, 5, 7, 4, 0)
+    tile_pass(plan_b, gs[0], False, 0, hand_on_one)
+    reduce_rows(0)
+    term = wt[r]
     for k in range(1, GROUP):
-        remote(wt_land.at[k], wt_land.at[k], w1_send.at[k], w1_recv.at[k], partner).wait_recv()
+        land = wt_land.at[k]
+        remote(land, land, w1_send.at[k], w1_recv.at[k], partner).wait_recv()
         term = term + wt_land[k]
     wpart[...] = term
     for k in range(1, GROUP):
         copy = remote(
-            wpart, wpart_land.at[k], w2_send.at[k], w2_recv.at[k], ((r + k) % GROUP, c)
+            wpart, wpart_land.at[k], w2_send.at[k], w2_recv.at[k], (r, (c + k) % GROUP)
         )
         copy.start()
         pending.append(copy)
-    slot = gs.at[pl.ds(2 * (2 * z + 1 - xhi), 2)]
-    remote(slot, slot, ag2_send.at[0], ag2_recv.at[0], partner).wait_recv()
-    for k in ahead:
-        slot = gs.at[pl.ds(2 * (2 * z_at(k, -1) + 1 - xhi), 2)]
-        remote(slot, slot, ag2f_send.at[k - 1], ag2f_recv.at[k - 1], partner).wait_recv()
-
-    tile_pass(plan_b, gs, False)
-    order = (2, 6, 1, 3, 5, 7, 4, 0)
-    for k in order:
+    gathered(1)
+
+    def finish_weight(turn):
+        @pl.when(turn == TURNS // 2)
+        def _():
+            term = wpart[...]
+            for k in range(1, GROUP):
+                land = wpart_land.at[k]
+                remote(land, land, w2_send.at[k], w2_recv.at[k], partner).wait_recv()
+                term = term + wpart_land[k]
+            wgrad_v[r] = term * (1.0 / math.sqrt(SIDE * BLOCKS * GROUP))
+            for k in range(1, GROUP):
+                slot = wgrad_v.at[r]
+                remote(slot, slot, w3_send.at[k], w3_recv.at[k], ((r + k) % GROUP, c)).start()
+
+    tile_pass(plan_b, gs[1], False, 1, finish_weight)
+    reduce_rows(1)
+    for k in range(1, GROUP):
+        slot = wgrad_v.at[(r - k + GROUP) % GROUP]
+        copy = remote(slot, slot, w3_send.at[k], w3_recv.at[k], ((r + k) % GROUP, c))
+        copy.wait_recv()
+        pending.append(copy)
+    wgrad_out = pltpu.make_async_copy(wgrad_v, wgrad_hbm, out_sem.at[2])
+    wgrad_out.start()
+
+    own = [fgrad_t[h] for h in range(2)]
+    for k in (1, 3, 4, 2, 5, 7, 6):
+        for f in range(2):
+            land = row_land.at[f, k]
+            remote(land, land, rsr_send.at[f, k], rsr_recv.at[f, k], sibling).wait_recv()
         for h in range(2):
-            b = 2 * (2 * chip_at(k, 1) + 1 - core) + h
-            row_out[k, h] = block_sum(plan_b, b).astype(BF16)
-        copy = remote(row_out.at[k], row_in.at[k], rsc_send.at[k], rsc_recv.at[k], sibling)
-        copy.start()
-        pending.append(copy)
-    for k in order:
-        mine = [block_sum(plan_b, 2 * (2 * chip_at(k, 1) + core) + h) for h in range(2)]
-        remote(row_in.at[k], row_in.at[k], rsc_send.at[k], rsc_recv.at[k], sibling).wait_recv()
-        mine = [mine[h] + row_in[k, h].astype(F32) for h in range(2)]
-        if k == 0:
-            own = mine
-        else:
-            for h in range(2):
-                row_sum[k, h] = mine[h].astype(BF16)
-            copy = remote(
-                row_sum.at[k], row_land.at[k], rsr_send.at[k - 1], rsr_recv.at[k - 1],
-                (2 * chip_at(k, 1) + core, c),
-            )
-            copy.start()
-            pending.append(copy)
-
-    term = wpart[...]
-    for k in range(1, GROUP):
-        remote(wpart_land.at[k], wpart_land.at[k], w2_send.at[k], w2_recv.at[k], partner).wait_recv()
-        term = term + wpart_land[k]
-    wgrad_v[c] = term * (1.0 / math.sqrt(SIDE * BLOCKS * GROUP))
-    for k in range(1, GROUP):
-        copy = remote(
-            wgrad_v.at[c], wgrad_v.at[c], w3_send.at[k], w3_recv.at[k], (r, (c + k) % GROUP)
-        )
-        copy.start()
-        pending.append(copy)
-
-    for k in (1, 3, 4, 2, 5, 7, 6):
-        remote(
-            row_land.at[k], row_land.at[k], rsr_send.at[k - 1], rsr_recv.at[k - 1], sibling
-        ).wait_recv()
-        own = [own[h] + row_land[k, h].astype(F32) for h in range(2)]
+            parts = [row_land[f, k, h].astype(F32) for f in range(2)]
+            own[h] = own[h] + jnp.concatenate(parts, axis=0)
     for h in range(2):
         fgrad_v[h * SIDE : (h + 1) * SIDE, :] = own[h].T.astype(BF16)
     fgrad_out = pltpu.make_async_copy(fgrad_v, fgrad_hbm, out_sem.at[1])
     fgrad_out.start()
-    for k in range(1, GROUP):
-        slot = wgrad_v.at[(c - k + GROUP) % GROUP]
-        remote(slot, slot, w3_send.at[k], w3_recv.at[k], partner).wait_recv()
-    wgrad_out = pltpu.make_async_copy(wgrad_v, wgrad_hbm, out_sem.at[2])
-    wgrad_out.start()
     for copy in pending:
         copy.wait_send()
     act_out.wait()
@@ -338,7 +385,9 @@
     hidden = weight.shape[1]
     any_spec = pl.BlockSpec(memory_space=pl.ANY)
     dma = pltpu.SemaphoreType.DMA
+    in_hbm = lambda array: pltpu.with_memory_space_constraint(array, pltpu.HBM)
     blocks = lambda *lead: pltpu.VMEM((*lead, SIDE, SIDE), BF16)
+    halves = lambda *lead: pltpu.VMEM((*lead, HALF, SIDE), BF16)
     act, fgrad, wgrad = pl.pallas_call(
         kernel,
         out_shape=(
@@ -352,7 +401,8 @@
             blocks(SLOTS),
             pltpu.VMEM((PAIRS, SIDE, SIDE), F32),
             blocks(BLOCKS + 1),
-            blocks(BLOCKS + 1),
+            halves(BLOCKS + 1),
+            halves(BLOCKS + 1),
             pltpu.VMEM((width, hidden), BF16),
             pltpu.VMEM((nodes, hidden), BF16),
             pltpu.VMEM((1, SLOTS), jnp.int32),
@@ -361,7 +411,8 @@
             pltpu.VMEM((nodes, hidden), BF16),
             pltpu.VMEM((nodes, width), BF16),
             blocks(8, 2), blocks(8, 2), blocks(8, 2), blocks(8, 2),
-            blocks(8, 2), blocks(8, 2), blocks(8, 2), blocks(8, 2),
+            halves(2, 8, 2), halves(2, 8, 2), halves(2, 8, 2), halves(2, 8, 2),
+            pltpu.VMEM((2, SIDE, SIDE), F32),
             pltpu.VMEM((GROUP, 8, hidden), F32),
             pltpu.VMEM((GROUP, 8, hidden), F32),
             pltpu.VMEM((8, hidden), F32),
@@ -373,8 +424,8 @@
             dma((LOADS,)), dma((6,)), dma((2,)), dma((3,)),
             dma((8,)), dma((8,)), dma((7,)), dma((7,)),
             dma((8,)), dma((8,)), dma((7,)), dma((7,)),
-            dma((8,)), dma((8,)), dma((7,)), dma((7,)),
-            dma((8,)), dma((8,)), dma((7,)), dma((7,)),
+            dma((2, 8)), dma((2, 8)), dma((2, 8)), dma((2, 8)),
+            dma((2, 8)), dma((2, 8)), dma((2, 8)), dma((2, 8)),
             dma((GROUP,)), dma((GROUP,)), dma((GROUP,)),
             dma((GROUP,)), dma((GROUP,)), dma((GROUP,)),
         ],
@@ -382,8 +433,8 @@
             collective_id=0, has_side_effects=True, vmem_limit_bytes=50 * 1024 * 1024
         ),
     )(
-        features.reshape(nodes // SIDE, SIDE, width), weight, adj_tiles,
-        tile_row, tile_col, tile_count, cotangent,
+        in_hbm(features.reshape(nodes // SIDE, SIDE, width)), in_hbm(weight), in_hbm(adj_tiles),
+        in_hbm(tile_row), in_hbm(tile_col), tile_count, in_hbm(cotangent),
     )
     return act, fgrad, wgrad.reshape(weight.shape)
 

time: 90.3 us -> 83 us (0.919)
  local copies, waits for them, and re-layouts: 5.88 us -> 1.94 us
  Pallas kernels: 82.4 us -> 79.6 us
    unnamed x13 -> x3, local copies, waits for them, and re-layouts: 5.88 us -> 1.94 us
    pallas_call x1, Pallas kernels: 82.4 us -> 79.6 us  [body(): pl.pallas_call(kernel, out_shape=(jax.ShapeDtypeStruct((nodes, hidden), B...]
where the time goes in v2:
time: 83 us; the launch traced here: 82.9 us
  Pallas kernels  79.6 us (96%)
  local copies, waits for them, and re-layouts  1.94 us (2%)
  between operations  1.29 us (2%)
    pallas_call x1, Pallas kernels, body(): pl.pallas_call(kernel, out_shape=(jax.ShapeDtypeStruct((nodes, hidden), B...  79.6 us
    unnamed x3, local copies, waits for them, and re-layouts  1.94 us

profile of v2, /device:TPU:1, one launch (start us, length us, event | category | flops | bytes accessed | tf_op | source)
XLA Modules:
  0.0 82.9 jit_solution(13405113759803826677)
XLA Ops:
  1.3 79.6 %shard_map.94 = (bf16[256,256]{1,0:T(8,128)(2,1)S(1)}, bf16[256,128]{1,0:T(8,128)(2,1)S(1)}, f32[16,8,256]{2,1,0:T(8,128)S(1)}) custom-call(bf16[2,128,128]{2,1,0:T(8,128)(2,1)} %bitcast.3, bf16[128,256]{1,0:T(8,128)(2,1)} %weight_hbm.1, bf16[1,1,384,128,128]{4,3,2,1,0:T(8,128)(2,1)} %adj_hbm.1, s32[1,1,384]{2,1,0:T(1,128)} %row_hbm.1, ...), custom_call_target="tpu_custom_call" | custom-call | tf_op jit(solution)/shard_map/pallas_call | solution.py:391
  80.9 0.7 copy.14
  81.6 0.6 copy.15
  82.2 0.7 copy.16

commit v3 on v2

v3 whole, which is shorter than its diff:
```python
import math

import jax
import jax.numpy as jnp
from jax import lax
from jax.experimental import pallas as pl
from jax.experimental.pallas import tpu as pltpu
from jax.sharding import PartitionSpec as P

F32 = jnp.float32
BF16 = jnp.bfloat16
MESH = pl.DeviceIdType.MESH

SIDE = 128
BLOCKS = 32
SLOTS = 384
PAIRS = (SLOTS + BLOCKS) // 2
ENTRIES = 512
GROUP = 16
HALF = SIDE // 2
UNROLL = 26
TURNS = PAIRS // UNROLL
EARLY = (5, 7)
LOADS = 8
ZERO = BLOCKS
TILE, SOURCE, KEEP, LAST, SOME = range(5)


def upright(flat, lanes):
    column = jnp.transpose(jnp.broadcast_to(flat, (SIDE, flat.shape[1])))
    return jnp.concatenate([column] * (lanes // SIDE), axis=1)


def over_rows(condition, value):
    return jnp.sum(jnp.where(condition, value, 0), axis=0, keepdims=True)


def plan_pairs(place, pick, total):
    def counts(shape):
        return [lax.broadcasted_iota(jnp.int32, shape, d) for d in range(2)]

    place_up = upright(place, SLOTS)
    down, across = counts((SLOTS, SLOTS))
    rank = over_rows((place_up == place) & (down < total) & (down < across), 1)
    down, across = counts((SLOTS, SIDE))
    tiles = over_rows((place_up[:, :SIDE] == across) & (down < total), 1)
    pairs = (tiles + 1) // 2
    pairs_up = upright(pairs, SIDE)
    down, across = counts((SIDE, SIDE))
    first = over_rows(down < across, pairs_up)
    first_up = upright(first, ENTRIES)
    down, across = counts((BLOCKS, SLOTS))
    spot = rank + 2 * over_rows(down == place, first_up[:BLOCKS, :SLOTS])
    spot = jnp.where(lax.broadcasted_iota(jnp.int32, (1, SLOTS), 1) < total, spot, -1)
    down, across = counts((SLOTS, ENTRIES))
    found = upright(spot, ENTRIES) == across
    tile = over_rows(found, down)
    source = over_rows(found, upright(pick, ENTRIES) - ZERO) + ZERO
    down, across = counts((BLOCKS, ENTRIES))
    pairs_up = jnp.concatenate([pairs_up[:BLOCKS]] * (ENTRIES // SIDE), axis=1)
    keep = 1 - over_rows((first_up[:BLOCKS] == across) & (pairs_up > 0), 1)
    return tile, source, keep, jnp.maximum(first + pairs - 1, 0), jnp.minimum(pairs, 1)


def kernel(
    feat_hbm, weight_hbm, adj_hbm, row_hbm, col_hbm, count_hbm, cot_hbm,
    act_hbm, fgrad_hbm, wgrad_hbm,
    tiles, sums, xs, gs_a, gs_b, weight, cot, rows, cols, plan_v, act_v, fgrad_v,
    col_out, col_in, col_sum, col_land, row_out, row_in, row_sum, row_land,
    agg_own, fgrad_t, wt, wt_land, wpart, wpart_land, wgrad_v,
    plan_f, plan_b, count,
    load_sem, small_sem, plan_sem, out_sem,
    ag1_send, ag1_recv, ag1f_send, ag1f_recv,
    rsx_send, rsx_recv, rsz_send, rsz_recv,
    ag2_send, ag2_recv, ag2f_send, ag2f_recv,
    rsc_send, rsc_recv, rsr_send, rsr_recv,
    w_send, w_recv,
):
    r = lax.axis_index("row")
    c = lax.axis_index("col")
    core, chip = r % 2, r // 2
    xlo, y = chip // 4, chip % 4
    xhi, z = c % 2, c // 2
    sibling = (2 * chip + (1 - core), c)
    partner = (r, 2 * z + (1 - xhi))
    gs = (gs_a, gs_b)

    def chip_at(k, sign):
        return 4 * ((xlo + k // 4) % 2) + (y + sign * (k % 4) + 4) % 4

    def z_at(k, sign):
        return (z + sign * k + 8) % 8

    def remote(src, dst, send, recv, device):
        return pltpu.make_async_remote_copy(
            src_ref=src, dst_ref=dst, send_sem=send, recv_sem=recv,
            device_id=device, device_id_type=MESH,
        )

    def all_sent(whole, sem):
        remote(whole, whole, sem, sem, partner).wait_send()

    def all_here(whole, sem):
        remote(whole, whole, sem, sem, partner).wait_recv()

    barrier = pltpu.get_barrier_semaphore()
    for k in range(1, GROUP):
        pl.semaphore_signal(barrier, inc=1, device_id=((r + k) % GROUP, c), device_id_type=MESH)
        pl.semaphore_signal(barrier, inc=1, device_id=(r, (c + k) % GROUP), device_id_type=MESH)

    smalls = [
        pltpu.make_async_copy(row_hbm.at[0, 0], rows.at[0], small_sem.at[0]),
        pltpu.make_async_copy(col_hbm.at[0, 0], cols.at[0], small_sem.at[1]),
        pltpu.make_async_copy(count_hbm, count, small_sem.at[2]),
        pltpu.make_async_copy(feat_hbm, xs.at[pl.ds(2 * r, 2)], small_sem.at[3]),
        pltpu.make_async_copy(weight_hbm, weight, small_sem.at[4]),
        pltpu.make_async_copy(cot_hbm, cot, small_sem.at[5]),
    ]
    for copy in smalls:
        copy.start()
    part = SLOTS // LOADS
    loads = [
        pltpu.make_async_copy(
            adj_hbm.at[0, 0, pl.ds(i * part, part)], tiles.at[pl.ds(i * part, part)], load_sem.at[i]
        )
        for i in range(LOADS)
    ]
    for copy in loads:
        copy.start()
    xs[ZERO] = jnp.zeros((SIDE, SIDE), BF16)
    for f in range(2):
        gs[f][ZERO] = jnp.zeros((HALF, SIDE), BF16)
    pl.semaphore_wait(barrier, 2 * (GROUP - 1))

    here = pl.ds(2 * r, 2)
    for k in (1, 4, 3, 5, 7, 2, 6, 0):
        device = sibling if k == 0 else (2 * chip_at(k, 1) + core, c)
        remote(feat_hbm, xs.at[here], ag1_send, ag1_recv.at[k], device).start()

    for copy in smalls[:3]:
        copy.wait()
    total = count[0, 0]
    plan_v[...] = jnp.zeros_like(plan_v)
    for i, (place, pick, ready) in enumerate(((rows, cols, plan_f), (cols, rows, plan_b))):
        listed = plan_pairs(place[...], pick[...], total)
        for j, value in enumerate(listed):
            plan_v[i, j : j + 1, : value.shape[1]] = value
        pltpu.make_async_copy(plan_v.at[i], ready, plan_sem.at[i]).start()

    for k in (1, 4, 3, 5, 7, 2, 6):
        slot = xs.at[pl.ds(2 * (2 * chip_at(k, -1) + core), 2)]
        remote(slot, slot, ag1_send, ag1_recv.at[k], sibling).wait_recv()
        remote(slot, slot, ag1f_send, ag1f_recv, sibling).start()
    slot = xs.at[pl.ds(2 * (2 * chip + 1 - core), 2)]
    remote(slot, slot, ag1_send, ag1_recv.at[0], sibling).wait_recv()
    for copy in smalls[3:]:
        copy.wait()
    for i in range(2):
        pltpu.make_async_copy(plan_v.at[i], (plan_f, plan_b)[i], plan_sem.at[i]).wait()
    for copy in loads:
        copy.wait()
    all_sent(xs.at[pl.ds(0, 16)], ag1_send)
    all_here(xs.at[pl.ds(0, 14)], ag1f_recv)

    def rows_of(half):
        return pl.ds(half * HALF, HALF)

    def tile_pass(listed, source, forward, half, service):
        here = rows_of(half)

        def some_pairs(turn, total):
            for u in range(UNROLL):
                p = turn * UNROLL + u
                with_one, with_two = source[listed[SOURCE, 2 * p]], source[listed[SOURCE, 2 * p + 1]]
                if forward:
                    one, two = tiles[listed[TILE, 2 * p], here], tiles[listed[TILE, 2 * p + 1], here]
                    left = jnp.concatenate([one, two], axis=1)
                    right = jnp.concatenate([with_one, with_two], axis=0)
                else:
                    one, two = tiles[listed[TILE, 2 * p]], tiles[listed[TILE, 2 * p + 1]]
                    left = jnp.concatenate([with_one, with_two], axis=1)
                    right = jnp.concatenate([one, two], axis=0)
                product = jnp.dot(left, right, preferred_element_type=F32)
                total = total * listed[KEEP, p].astype(F32) + product
                sums[p, here, :] = total
            if service is not None:
                service(turn)
            return total

        lax.fori_loop(0, TURNS, some_pairs, jnp.zeros((HALF, SIDE), F32))

    def block_sum(listed, b, here):
        return sums[listed[LAST, b], here, :] * listed[SOME, b].astype(F32)

    order = (4, 3, 5, 2, 6, 1, 7, 0)

    def send_columns(f):
        for k in order:
            for h in range(2):
                b = 2 * (2 * z_at(k, 1) + 1 - xhi) + h
                col_out[f, k, h] = block_sum(plan_f, b, rows_of(f)).astype(BF16)
            remote(
                col_out.at[f, k], col_in.at[f, k], rsx_send.at[f], rsx_recv.at[f, k], partner
            ).start()

    def pass_columns(f, k):
        blocks = [2 * (2 * z_at(k, 1) + xhi) + h for h in range(2)]
        mine = [block_sum(plan_f, b, rows_of(f)) for b in blocks]
        come = col_in.at[f, k]
        remote(come, come, rsx_send.at[f], rsx_recv.at[f, k], partner).wait_recv()
        for h in range(2):
            both = mine[h] + col_in[f, k, h].astype(F32)
            if k == 0:
                agg_own[h, rows_of(f), :] = both
            else:
                col_sum[f, k - 1, h] = both.astype(BF16)
        if k != 0:
            remote(
                col_sum.at[f, k - 1], col_land.at[f, k - 1], rsz_send.at[f], rsz_recv.at[f],
                (r, 2 * z_at(k, 1) + xhi),
            ).start()

    def begin_columns(turn):
        for i, at in enumerate(EARLY):
            @pl.when(turn == at)
            def _():
                pass_columns(0, order[i])

    tile_pass(plan_f, xs, True, 0, None)
    send_columns(0)
    tile_pass(plan_f, xs, True, 1, begin_columns)
    send_columns(1)
    for k in order[len(EARLY) :]:
        pass_columns(0, k)
    for k in order:
        pass_columns(1, k)
    all_sent(xs.at[pl.ds(0, 14)], ag1f_send)
    for f in range(2):
        all_sent(col_out.at[f], rsx_send.at[f])
    for f in range(2):
        all_here(col_land.at[f], rsz_recv.at[f])
    own = [agg_own[h] for h in range(2)]
    for k in range(7):
        for h in range(2):
            parts = [col_land[f, k, h].astype(F32) for f in range(2)]
            own[h] = own[h] + jnp.concatenate(parts, axis=0)

    aggregated = jnp.concatenate(own, axis=0).astype(BF16)
    w = weight[...]
    preact = jnp.dot(aggregated, w, preferred_element_type=F32)
    sigma = jax.nn.sigmoid(preact)
    slope = sigma * (1.0 + preact * (1.0 - sigma))
    pre_grad = (cot[...].astype(F32) * slope).astype(BF16)
    agg_grad = lax.dot_general(
        w, pre_grad, (((1,), (1,)), ((), ())), preferred_element_type=F32
    ).astype(BF16)
    for f in range(2):
        for h in range(2):
            gs[f][2 * c + h] = agg_grad[f * HALF : (f + 1) * HALF, h * SIDE : (h + 1) * SIDE]

    def nodes_of(at, other):
        across = 1 - xhi if other else xhi
        return pl.ds(2 * (2 * at + across), 2)

    def spread(f, k):
        slot = gs[f].at[nodes_of(z, False)]
        if k == 0:
            remote(slot, slot, ag2_send.at[f], ag2f_recv.at[f], partner).start()
        else:
            device = (r, 2 * z_at(k, 1) + xhi)
            remote(slot, slot, ag2_send.at[f], ag2_recv.at[f, k], device).start()

    def hand_on(f, k):
        slot = gs[f].at[nodes_of(z_at(k, -1), False)]
        remote(slot, slot, ag2_send.at[f], ag2_recv.at[f, k], partner).wait_recv()
        remote(slot, slot, ag2f_send.at[f], ag2f_recv.at[f], partner).start()

    ahead = (1, 7, 2, 6, 3, 5, 4)
    for k in ahead + (0,):
        spread(0, k)

    act_v[...] = (preact * sigma).astype(BF16)
    act_out = pltpu.make_async_copy(act_v, act_hbm, out_sem.at[0])
    act_out.start()
    terms = lax.dot_general(
        aggregated, pre_grad, (((0,), (0,)), ((), ())), preferred_element_type=F32
    )
    for q in range(GROUP):
        wt[q] = terms[8 * q : 8 * q + 8]
    for k in range(1, GROUP):
        to = (r + k) % GROUP
        remote(wt.at[to], wt_land.at[k - 1], w_send.at[0], w_recv.at[0], (to, c)).start()

    for k in ahead:
        hand_on(0, k)
        spread(1, k)
    spread(1, 0)
    for f in range(2):
        all_sent(col_sum.at[f], rsz_send.at[f])
    all_here(gs[0].at[pl.ds(0, 16)], ag2f_recv.at[0])

    def hand_on_one(turn):
        @pl.when(turn < 7)
        def _():
            step = turn // 2
            hand_on(1, (1 - turn % 2) * (step + 1) + (turn % 2) * (7 - step))

    def reduce_rows(f):
        for k in turns:
            for h in range(2):
                b = 2 * (2 * chip_at(k, 1) + 1 - core) + h
                row_out[f, k, h] = block_sum(plan_b, b, rows_of(f)).astype(BF16)
            remote(
                row_out.at[f, k], row_in.at[f, k], rsc_send.at[f], rsc_recv.at[f, k], sibling
            ).start()
        for k in turns:
            blocks = [2 * (2 * chip_at(k, 1) + core) + h for h in range(2)]
            mine = [block_sum(plan_b, b, rows_of(f)) for b in blocks]
            come = row_in.at[f, k]
            remote(come, come, rsc_send.at[f], rsc_recv.at[f, k], sibling).wait_recv()
            for h in range(2):
                both = mine[h] + row_in[f, k, h].astype(F32)
                if k == 0:
                    fgrad_t[h, rows_of(f), :] = both
                else:
                    row_sum[f, k - 1, h] = both.astype(BF16)
            if k != 0:
                remote(
                    row_sum.at[f, k - 1], row_land.at[f, k - 1], rsr_send.at[f], rsr_recv.at[f],
                    (2 * chip_at(k, 1) + core, c),
                ).start()

    turns = (2, 6, 1, 3, 5, 7, 4, 0)
    tile_pass(plan_b, gs[0], False, 0, hand_on_one)
    reduce_rows(0)
    all_here(wt_land, w_recv.at[0])
    term = wt[r]
    for k in range(GROUP - 1):
        term = term + wt_land[k]
    wpart[...] = term
    for k in range(1, GROUP):
        device = (r, (c + k) % GROUP)
        remote(wpart, wpart_land.at[k - 1], w_send.at[1], w_recv.at[1], device).start()
    all_here(gs[1].at[pl.ds(0, 16)], ag2f_recv.at[1])

    def finish_weight(turn):
        @pl.when(turn == TURNS // 2)
        def _():
            all_here(wpart_land, w_recv.at[1])
            term = wpart[...]
            for k in range(GROUP - 1):
                term = term + wpart_land[k]
            wgrad_v[r] = term * (1.0 / math.sqrt(SIDE * BLOCKS * GROUP))
            slot = wgrad_v.at[r]
            for k in range(1, GROUP):
                remote(slot, slot, w_send.at[2], w_recv.at[2], ((r + k) % GROUP, c)).start()

    tile_pass(plan_b, gs[1], False, 1, finish_weight)
    reduce_rows(1)
    others = pl.ds(0, GROUP - 1)
    all_here(wgrad_v.at[others], w_recv.at[2])
    wgrad_out = pltpu.make_async_copy(wgrad_v, wgrad_hbm, out_sem.at[2])
    wgrad_out.start()
    for i in range(3):
        all_sent(wt.at[others], w_send.at[i])
    for f in range(2):
        all_sent(gs[f].at[pl.ds(0, 16)], ag2_send.at[f])
        all_sent(gs[f].at[pl.ds(0, 14)], ag2f_send.at[f])
        all_sent(row_out.at[f], rsc_send.at[f])
    act_out.wait()

    own = [fgrad_t[h] for h in range(2)]
    for f in range(2):
        all_here(row_land.at[f], rsr_recv.at[f])
    for k in range(7):
        for h in range(2):
            parts = [row_land[f, k, h].astype(F32) for f in range(2)]
            own[h] = own[h] + jnp.concatenate(parts, axis=0)
    for h in range(2):
        fgrad_v[h * SIDE : (h + 1) * SIDE, :] = own[h].T.astype(BF16)
    fgrad_out = pltpu.make_async_copy(fgrad_v, fgrad_hbm, out_sem.at[1])
    fgrad_out.start()
    for f in range(2):
        all_sent(row_sum.at[f], rsr_send.at[f])
    wgrad_out.wait()
    fgrad_out.wait()


def body(features, weight, adj_tiles, tile_row, tile_col, tile_count, cotangent):
    nodes, width = features.shape
    hidden = weight.shape[1]
    any_spec = pl.BlockSpec(memory_space=pl.ANY)
    dma = pltpu.SemaphoreType.DMA
    in_hbm = lambda array: pltpu.with_memory_space_constraint(array, pltpu.HBM)
    blocks = lambda *lead: pltpu.VMEM((*lead, SIDE, SIDE), BF16)
    halves = lambda *lead: pltpu.VMEM((*lead, HALF, SIDE), BF16)
    act, fgrad, wgrad = pl.pallas_call(
        kernel,
        out_shape=(
            jax.ShapeDtypeStruct((nodes, hidden), BF16),
            jax.ShapeDtypeStruct((nodes, width), BF16),
            jax.ShapeDtypeStruct((GROUP, 8, hidden), F32),
        ),
        in_specs=[any_spec] * 7,
        out_specs=(any_spec,) * 3,
        scratch_shapes=[
            blocks(SLOTS),
            pltpu.VMEM((PAIRS, SIDE, SIDE), F32),
            blocks(BLOCKS + 1),
            halves(BLOCKS + 1),
            halves(BLOCKS + 1),
            pltpu.VMEM((width, hidden), BF16),
            pltpu.VMEM((nodes, hidden), BF16),
            pltpu.VMEM((1, SLOTS), jnp.int32),
            pltpu.VMEM((1, SLOTS), jnp.int32),
            pltpu.VMEM((2, 8, ENTRIES), jnp.int32),
            pltpu.VMEM((nodes, hidden), BF16),
            pltpu.VMEM((nodes, width), BF16),
            halves(2, 8, 2), halves(2, 8, 2), halves(2, 7, 2), halves(2, 7, 2),
            halves(2, 8, 2), halves(2, 8, 2), halves(2, 7, 2), halves(2, 7, 2),
            pltpu.VMEM((2, SIDE, SIDE), F32),
            pltpu.VMEM((2, SIDE, SIDE), F32),
            pltpu.VMEM((GROUP, 8, hidden), F32),
            pltpu.VMEM((GROUP - 1, 8, hidden), F32),
            pltpu.VMEM((8, hidden), F32),
            pltpu.VMEM((GROUP - 1, 8, hidden), F32),
            pltpu.VMEM((GROUP, 8, hidden), F32),
            pltpu.SMEM((8, ENTRIES), jnp.int32),
            pltpu.SMEM((8, ENTRIES), jnp.int32),
            pltpu.SMEM((1, 1), jnp.int32),
            dma((LOADS,)), dma((6,)), dma((2,)), dma((3,)),
            dma, dma((8,)), dma, dma,
            dma((2,)), dma((2, 8)), dma((2,)), dma((2,)),
            dma((2,)), dma((2, 8)), dma((2,)), dma((2,)),
            dma((2,)), dma((2, 8)), dma((2,)), dma((2,)),
            dma((3,)), dma((3,)),
        ],
        compiler_params=pltpu.CompilerParams(
            collective_id=0, has_side_effects=True, vmem_limit_bytes=50 * 1024 * 1024
        ),
    )(
        in_hbm(features.reshape(nodes // SIDE, SIDE, width)), in_hbm(weight), in_hbm(adj_tiles),
        in_hbm(tile_row), in_hbm(tile_col), tile_count, in_hbm(cotangent),
    )
    return act, fgrad, wgrad.reshape(weight.shape)


def solution(mesh):
    in_specs = (
        P(("col", "row"), None),
        P(),
        P("row", "col", None, None, None),
        P("row", "col", None),
        P("row", "col", None),
        P("row", "col"),
        P(("row", "col"), None),
    )
    out_specs = (P(("row", "col"), None), P(("col", "row"), None), P())
    return jax.shard_map(body, mesh=mesh, in_specs=in_specs, out_specs=out_specs, check_vma=False)
```

time: 83 us -> 78.5 us (0.946)
  Pallas kernels: 79.6 us -> 75.2 us
    pallas_call x1, Pallas kernels: 79.6 us -> 75.2 us  [body(): pl.pallas_call(kernel, out_shape=(jax.ShapeDtypeStruct((nodes, hidden), B...]
where the time goes in v3:
time: 78.5 us; the launch traced here: 78.4 us
  Pallas kernels  75.2 us (96%)
  local copies, waits for them, and re-layouts  1.94 us (2%)
  between operations  1.29 us (2%)
    pallas_call x1, Pallas kernels, body(): pl.pallas_call(kernel, out_shape=(jax.ShapeDtypeStruct((nodes, hidden), B...  75.2 us
    unnamed x3, local copies, waits for them, and re-layouts  1.94 us

profile of v3, /device:TPU:1, one launch (start us, length us, event | category | flops | bytes accessed | tf_op | source)
XLA Modules:
  0.0 78.4 jit_solution(356536152755226637)
XLA Ops:
  1.3 75.2 %shard_map.94 = (bf16[256,256]{1,0:T(8,128)(2,1)S(1)}, bf16[256,128]{1,0:T(8,128)(2,1)S(1)}, f32[16,8,256]{2,1,0:T(8,128)S(1)}) custom-call(bf16[2,128,128]{2,1,0:T(8,128)(2,1)} %bitcast.3, bf16[128,256]{1,0:T(8,128)(2,1)} %weight_hbm.1, bf16[1,1,384,128,128]{4,3,2,1,0:T(8,128)(2,1)} %adj_hbm.1, s32[1,1,384]{2,1,0:T(1,128)} %row_hbm.1, ...), custom_call_target="tpu_custom_call" | custom-call | tf_op jit(solution)/shard_map/pallas_call | solution.py:397
  76.5 0.7 copy.14
  77.2 0.6 copy.15
  77.8 0.7 copy.16

commit v4 on v3

--- a/solution.py
+++ b/solution.py
@@ -19,6 +19,7 @@
 GROUP = 16
 HALF = SIDE // 2
 UNROLL = 26
+LONG = 104
 TURNS = PAIRS // UNROLL
 EARLY = (5, 7)
 LOADS = 8
@@ -67,7 +68,7 @@
     act_hbm, fgrad_hbm, wgrad_hbm,
     tiles, sums, xs, gs_a, gs_b, weight, cot, rows, cols, plan_v, act_v, fgrad_v,
     col_out, col_in, col_sum, col_land, row_out, row_in, row_sum, row_land,
-    agg_own, fgrad_t, wt, wt_land, wpart, wpart_land, wgrad_v,
+    agg_own, fgrad_t, wt, wt_land, wpart, wnear, wpart_land, wgrad_v,
     plan_f, plan_b, count,
     load_sem, small_sem, plan_sem, out_sem,
     ag1_send, ag1_recv, ag1f_send, ag1f_recv,
@@ -166,11 +167,12 @@
         return pl.ds(half * HALF, HALF)
 
     def tile_pass(listed, source, forward, half, service):
+        unroll = LONG if service is None else UNROLL
         here = rows_of(half)
 
         def some_pairs(turn, total):
-            for u in range(UNROLL):
-                p = turn * UNROLL + u
+            for u in range(unroll):
+                p = turn * unroll + u
                 with_one, with_two = source[listed[SOURCE, 2 * p]], source[listed[SOURCE, 2 * p + 1]]
                 if forward:
                     one, two = tiles[listed[TILE, 2 * p], here], tiles[listed[TILE, 2 * p + 1], here]
@@ -187,7 +189,7 @@
                 service(turn)
             return total
 
-        lax.fori_loop(0, TURNS, some_pairs, jnp.zeros((HALF, SIDE), F32))
+        lax.fori_loop(0, PAIRS // unroll, some_pairs, jnp.zeros((HALF, SIDE), F32))
 
     def block_sum(listed, b, here):
         return sums[listed[LAST, b], here, :] * listed[SOME, b].astype(F32)
@@ -276,12 +278,16 @@
         remote(slot, slot, ag2f_send.at[f], ag2f_recv.at[f], partner).start()
 
     ahead = (1, 7, 2, 6, 3, 5, 4)
-    for k in ahead + (0,):
+    for k in (0,) + ahead:
         spread(0, k)
+    spread(1, 0)
 
     act_v[...] = (preact * sigma).astype(BF16)
     act_out = pltpu.make_async_copy(act_v, act_hbm, out_sem.at[0])
     act_out.start()
+    for k in ahead:
+        hand_on(0, k)
+        spread(1, k)
     terms = lax.dot_general(
         aggregated, pre_grad, (((0,), (0,)), ((), ())), preferred_element_type=F32
     )
@@ -290,11 +296,6 @@
     for k in range(1, GROUP):
         to = (r + k) % GROUP
         remote(wt.at[to], wt_land.at[k - 1], w_send.at[0], w_recv.at[0], (to, c)).start()
-
-    for k in ahead:
-        hand_on(0, k)
-        spread(1, k)
-    spread(1, 0)
     for f in range(2):
         all_sent(col_sum.at[f], rsz_send.at[f])
     all_here(gs[0].at[pl.ds(0, 16)], ag2f_recv.at[0])
@@ -338,31 +339,30 @@
     for k in range(GROUP - 1):
         term = term + wt_land[k]
     wpart[...] = term
+    wnear[...] = jnp.concatenate([term[:, :SIDE], term[:, SIDE:]], axis=0).astype(BF16)
     for k in range(1, GROUP):
         device = (r, (c + k) % GROUP)
-        remote(wpart, wpart_land.at[k - 1], w_send.at[1], w_recv.at[1], device).start()
+        remote(wnear, wpart_land.at[k - 1], w_send.at[1], w_recv.at[1], device).start()
     all_here(gs[1].at[pl.ds(0, 16)], ag2f_recv.at[1])
 
-    def finish_weight(turn):
-        @pl.when(turn == TURNS // 2)
-        def _():
-            all_here(wpart_land, w_recv.at[1])
-            term = wpart[...]
-            for k in range(GROUP - 1):
-                term = term + wpart_land[k]
-            wgrad_v[r] = term * (1.0 / math.sqrt(SIDE * BLOCKS * GROUP))
-            slot = wgrad_v.at[r]
-            for k in range(1, GROUP):
-                remote(slot, slot, w_send.at[2], w_recv.at[2], ((r + k) % GROUP, c)).start()
-
-    tile_pass(plan_b, gs[1], False, 1, finish_weight)
+    tile_pass(plan_b, gs[1], False, 1, None)
     reduce_rows(1)
+
+    all_here(wpart_land, w_recv.at[1])
+    far = wpart_land[0].astype(F32)
+    for k in range(1, GROUP - 1):
+        far = far + wpart_land[k].astype(F32)
+    term = wpart[...] + jnp.concatenate([far[:8], far[8:]], axis=1)
+    wgrad_v[r] = term * (1.0 / math.sqrt(SIDE * BLOCKS * GROUP))
+    for k in range(1, GROUP):
+        slot = wgrad_v.at[r]
+        remote(slot, slot, w_send.at[2], w_recv.at[2], ((r + k) % GROUP, c)).start()
     others = pl.ds(0, GROUP - 1)
     all_here(wgrad_v.at[others], w_recv.at[2])
     wgrad_out = pltpu.make_async_copy(wgrad_v, wgrad_hbm, out_sem.at[2])
     wgrad_out.start()
     for i in range(3):
-        all_sent(wt.at[others], w_send.at[i])
+        all_sent(wpart_land if i == 1 else wt.at[others], w_send.at[i])
     for f in range(2):
         all_sent(gs[f].at[pl.ds(0, 16)], ag2_send.at[f])
         all_sent(gs[f].at[pl.ds(0, 14)], ag2f_send.at[f])
@@ -423,7 +423,8 @@
             pltpu.VMEM((GROUP, 8, hidden), F32),
             pltpu.VMEM((GROUP - 1, 8, hidden), F32),
             pltpu.VMEM((8, hidden), F32),
-            pltpu.VMEM((GROUP - 1, 8, hidden), F32),
+            pltpu.VMEM((16, SIDE), BF16),
+            pltpu.VMEM((GROUP - 1, 16, SIDE), BF16),
             pltpu.VMEM((GROUP, 8, hidden), F32),
             pltpu.SMEM((8, ENTRIES), jnp.int32),
             pltpu.SMEM((8, ENTRIES), jnp.int32),

time: 78.5 us -> 75.6 us (0.963)
  Pallas kernels: 75.2 us -> 72.3 us
    pallas_call x1, Pallas kernels: 75.2 us -> 72.3 us  [body(): pl.pallas_call(kernel, out_shape=(jax.ShapeDtypeStruct((nodes, hidden), B...]
where the time goes in v4:
time: 75.6 us; the launch traced here: 75.5 us
  Pallas kernels  72.3 us (96%)
  local copies, waits for them, and re-layouts  1.94 us (3%)
  between operations  1.29 us (2%)
    pallas_call x1, Pallas kernels, body(): pl.pallas_call(kernel, out_shape=(jax.ShapeDtypeStruct((nodes, hidden), B...  72.3 us
    unnamed x3, local copies, waits for them, and re-layouts  1.94 us

profile of v4, /device:TPU:1, one launch (start us, length us, event | category | flops | bytes accessed | tf_op | source)
XLA Modules:
  0.0 75.5 jit_solution(3911035511697869782)
XLA Ops:
  1.3 72.3 %shard_map.94 = (bf16[256,256]{1,0:T(8,128)(2,1)S(1)}, bf16[256,128]{1,0:T(8,128)(2,1)S(1)}, f32[16,8,256]{2,1,0:T(8,128)S(1)}) custom-call(bf16[2,128,128]{2,1,0:T(8,128)(2,1)} %bitcast.3, bf16[128,256]{1,0:T(8,128)(2,1)} %weight_hbm.1, bf16[1,1,384,128,128]{4,3,2,1,0:T(8,128)(2,1)} %adj_hbm.1, s32[1,1,384]{2,1,0:T(1,128)} %row_hbm.1, ...), custom_call_target="tpu_custom_call" | custom-call | tf_op jit(solution)/shard_map/pallas_call | solution.py:397
  73.6 0.7 copy.14
  74.2 0.6 copy.15
  74.9 0.7 copy.16

commit v5 on v4

--- a/solution.py
+++ b/solution.py
@@ -21,7 +21,7 @@
 UNROLL = 26
 LONG = 104
 TURNS = PAIRS // UNROLL
-EARLY = (5, 7)
+EARLY = (2, 3)
 LOADS = 8
 ZERO = BLOCKS
 TILE, SOURCE, KEEP, LAST, SOME = range(5)
@@ -166,8 +166,7 @@
     def rows_of(half):
         return pl.ds(half * HALF, HALF)
 
-    def tile_pass(listed, source, forward, half, service):
-        unroll = LONG if service is None else UNROLL
+    def tile_pass(listed, source, forward, half, service, unroll=LONG):
         here = rows_of(half)
 
         def some_pairs(turn, total):
@@ -230,7 +229,7 @@
 
     tile_pass(plan_f, xs, True, 0, None)
     send_columns(0)
-    tile_pass(plan_f, xs, True, 1, begin_columns)
+    tile_pass(plan_f, xs, True, 1, begin_columns, 2 * UNROLL)
     send_columns(1)
     for k in order[len(EARLY) :]:
         pass_columns(0, k)
@@ -332,7 +331,7 @@
                 ).start()
 
     turns = (2, 6, 1, 3, 5, 7, 4, 0)
-    tile_pass(plan_b, gs[0], False, 0, hand_on_one)
+    tile_pass(plan_b, gs[0], False, 0, hand_on_one, UNROLL)
     reduce_rows(0)
     all_here(wt_land, w_recv.at[0])
     term = wt[r]

time: 75.6 us -> 75.5 us (level)
  no operation moved by 1% of the time
where the time goes in v5:
time: 75.5 us; the launch traced here: 75.4 us
  Pallas kernels  72.2 us (96%)
  local copies, waits for them, and re-layouts  1.94 us (3%)
  between operations  1.29 us (2%)
    pallas_call x1, Pallas kernels, body(): pl.pallas_call(kernel, out_shape=(jax.ShapeDtypeStruct((nodes, hidden), B...  72.2 us
    unnamed x3, local copies, waits for them, and re-layouts  1.94 us

profile of v5, /device:TPU:1, one launch (start us, length us, event | category | flops | bytes accessed | tf_op | source)
XLA Modules:
  0.0 75.4 jit_solution(15073204367594388518)
XLA Ops:
  1.3 72.2 %shard_map.94 = (bf16[256,256]{1,0:T(8,128)(2,1)S(1)}, bf16[256,128]{1,0:T(8,128)(2,1)S(1)}, f32[16,8,256]{2,1,0:T(8,128)S(1)}) custom-call(bf16[2,128,128]{2,1,0:T(8,128)(2,1)} %bitcast.3, bf16[128,256]{1,0:T(8,128)(2,1)} %weight_hbm.1, bf16[1,1,384,128,128]{4,3,2,1,0:T(8,128)(2,1)} %adj_hbm.1, s32[1,1,384]{2,1,0:T(1,128)} %row_hbm.1, ...), custom_call_target="tpu_custom_call" | custom-call | tf_op jit(solution)/shard_map/pallas_call | solution.py:396
  73.4 0.7 copy.14
  74.1 0.6 copy.15
  74.7 0.7 copy.16
